TPU v7x, 512 devices: a whole 4x8x8 slice. The times are simulated.
512 devices in a mesh: dp: 32 (over x, y), tensor: 16 (over z, core).
Axes of the slice: x: 4, y: 8, z: 8, core: 2. Of those that a mesh axis runs over, the one named last changes fastest.
Arguments:
- gradient: bfloat16 [24, 512, 512], P(None, 'dp', 'tensor'), may hold values from -6 to 6
- weight: bfloat16 [24, 512, 512], P(None, 'dp', 'tensor'), may hold values from -0.625 to 0.625
- owner_map: int32 [24, 1], replicated, may hold values from 0 to 15; in each aligned block of 24 rows (0 to 23, 24 to 47, ...) at most 3 rows name the same one
- stored_left_eigenvectors: bfloat16 [48, 512, 512], P('tensor'), may hold values from -0.25 to 0.25
- stored_right_eigenvectors: bfloat16 [48, 512, 512], P('tensor'), may hold values from -0.25 to 0.25
- left_gram: float32 [48, 512, 512], P('tensor', 'dp'), may hold values from -1024 to 1024, as said below
- right_gram: float32 [48, 512, 512], P('tensor', 'dp'), may hold values from -1024 to 1024, as said below
- rotated_first_moment: float32 [48, 512, 512], P('tensor', 'dp'), may hold values from -1.75 to 1.75
- rotated_second_moment: float32 [48, 512, 512], P('tensor', 'dp'), may hold values from 0.02 to 1
Outputs:
- new_weight: bfloat16 [24, 512, 512], P(None, None, 'tensor')
- new_left_gram: float32 [48, 512, 512], P('tensor', 'dp')
- new_right_gram: float32 [48, 512, 512], P('tensor', 'dp')
- new_first_moment: float32 [48, 512, 512], P('tensor', 'dp')
- new_second_moment: float32 [48, 512, 512], P('tensor', 'dp')
Inputs may be any that keep to these rules, and one draw needn't show every extreme that they name: `owner_map`: every tensor index owns at least one block and at most 3; some index owns exactly 3. `left_gram`: symmetric; diagonal entries between 256 and 1024. `right_gram`: symmetric; diagonal entries between 256 and 1024.
All inputs are finite; a program needn't handle non-finite values.
Results may differ from a plain program's by a relative error of at most 0.0021.
Values may be sent and summed in bfloat16 or wider, within the bound.
A program may use at most 64 MiB of HBM per device.

v0:
```python
import jax
import jax.numpy as jnp
from jax import lax
from jax.sharding import PartitionSpec as P

beta_one = 0.9
beta_two = 0.999
beta_gram = 0.95
epsilon = 1e-08
learn_rate = 0.01
decay_rate = 0.1


def slot_table(owner_map, slot_count, owners):
    owner_ids = owner_map[:, 0]
    blocks = owner_ids.shape[0]
    block_ids = jnp.arange(blocks, dtype=jnp.int32)
    before = block_ids[:, None] > block_ids[None, :]
    matches = owner_ids[:, None] == owner_ids[None, :]
    position = jnp.sum(jnp.where(before & matches, 1, 0), axis=1).astype(jnp.int32)
    target = owner_ids * slot_count + position
    slot_ids = jnp.arange(owners * slot_count, dtype=jnp.int32)
    return slot_ids[:, None] == target[None, :]


def per_device(
    gradient,
    weight,
    owner_map,
    stored_left_eigenvectors,
    stored_right_eigenvectors,
    left_gram,
    right_gram,
    rotated_first_moment,
    rotated_second_moment,
):
    slot_count = stored_left_eigenvectors.shape[0]
    rows_here = gradient.shape[1]
    cols_here = gradient.shape[2]
    owners = lax.axis_size("tensor")
    one_hot = slot_table(owner_map, slot_count, owners).astype(jnp.bfloat16)
    packed = jnp.einsum(
        "qb,bij->qij", one_hot, gradient, preferred_element_type=jnp.float32
    ).astype(jnp.bfloat16)
    packed = packed.reshape(owners, slot_count, rows_here, cols_here)
    received = lax.all_to_all(packed, "tensor", split_axis=0, concat_axis=3, tiled=True)[0]
    row_start = lax.axis_index("dp") * rows_here
    left_rows = lax.dynamic_slice_in_dim(stored_left_eigenvectors, row_start, rows_here, 1)
    left_cols = lax.dynamic_slice_in_dim(stored_left_eigenvectors, row_start, rows_here, 2)
    full_grad = lax.all_gather(received, "dp", axis=1, tiled=True)
    half_turn = jnp.einsum(
        "sij,sjk->sik", full_grad, stored_right_eigenvectors, preferred_element_type=jnp.float32
    ).astype(jnp.bfloat16)
    rotated = jnp.einsum("sji,sjk->sik", left_cols, half_turn, preferred_element_type=jnp.float32)
    moment_one = beta_one * rotated_first_moment + (1.0 - beta_one) * rotated
    moment_two = beta_two * rotated_second_moment + (1.0 - beta_two) * rotated * rotated
    direction = (moment_one / (jnp.sqrt(moment_two) + epsilon)).astype(jnp.bfloat16)
    full_direction = lax.all_gather(direction, "dp", axis=1, tiled=True)
    back_turn = jnp.einsum(
        "sij,skj->sik",
        full_direction,
        stored_right_eigenvectors,
        preferred_element_type=jnp.float32,
    ).astype(jnp.bfloat16)
    update = jnp.einsum(
        "sij,sjk->sik", left_rows, back_turn, preferred_element_type=jnp.float32
    ).astype(jnp.bfloat16)
    gram_scale = 1.0 - beta_gram
    new_left = beta_gram * left_gram + gram_scale * jnp.einsum(
        "sik,sjk->sij", received, full_grad, preferred_element_type=jnp.float32
    )
    grad_cols = lax.dynamic_slice_in_dim(full_grad, row_start, rows_here, 2)
    new_right = beta_gram * right_gram + gram_scale * jnp.einsum(
        "sji,sjk->sik", grad_cols, full_grad, preferred_element_type=jnp.float32
    )
    returned = lax.all_to_all(update[None], "tensor", split_axis=3, concat_axis=0, tiled=True)
    returned = returned.reshape(owners * slot_count, rows_here, cols_here)
    unpacked = jnp.einsum(
        "qb,qij->bij", one_hot, returned, preferred_element_type=jnp.float32
    ).astype(jnp.bfloat16)
    weight_wide = weight.astype(jnp.float32)
    stepped = (
        weight_wide - learn_rate * (unpacked.astype(jnp.float32) + decay_rate * weight_wide)
    ).astype(jnp.bfloat16)
    new_weight = lax.all_gather(stepped, "dp", axis=1, tiled=True)
    return (new_weight, new_left, new_right, moment_one, moment_two)


def solution(mesh):
    in_specs = (
        P(None, "dp", "tensor"),
        P(None, "dp", "tensor"),
        P(),
        P("tensor", None, None),
        P("tensor", None, None),
        P("tensor", "dp", None),
        P("tensor", "dp", None),
        P("tensor", "dp", None),
        P("tensor", "dp", None),
    )
    out_specs = (
        P(None, None, "tensor"),
        P("tensor", "dp", None),
        P("tensor", "dp", None),
        P("tensor", "dp", None),
        P("tensor", "dp", None),
    )
    return jax.shard_map(
        per_device, mesh=mesh, in_specs=in_specs, out_specs=out_specs, check_vma=False
    )
```

profile of v0, /device:TPU:6, one launch (start us, length us, event | category | flops | bytes accessed | tf_op | source)
XLA Modules:
  0.0 281.1 jit_solution(17534254796728118738)
XLA Ops:
  7.2 0.0 copy-start
  7.2 0.0 copy-start.5
  7.2 0.0 copy-start.6
  7.2 0.0 all-gather.3.cloned.1.call-start
  7.2 1.0 select_reduce_fusion
  8.2 0.7 multiply_add_fusion.1
  8.9 1.1 convolution_convert_fusion.2
  10.0 0.2 copy.43
  10.2 0.2 reshape.30
  10.4 18.0 %all_to_all.30 = bf16[16,2,768]{2,1,0:T(2,128)(2,1)S(1)} all-to-all(bf16[16,2,768]{2,1,0:T(2,128)(2,1)S(1)} %reshape.30), channel_id=1, replica_groups=mesh['dp'=32,'tensor'=16] {'tensor'}, dimensions={0} | all-to-all | bytes 98304 | tf_op jit(solution)/shard_map/all_to_all | solution.py:46
  28.4 0.1 reshape.31
  28.6 0.1 copy.44
  28.6 0.8 squeeze.7
  29.4 0.0 all-gather.3.cloned.1.call-update
  29.5 0.0 all-gather.5.cloned.1.call-start
  29.5 0.0 copy-start.2
  29.5 0.0 copy-start.3
  29.5 77.8 %all-gather.3.cloned.1.call-done = bf16[3,512,512]{2,1,0:T(8,128)(2,1)} async-done(((bf16[3,16,512]{2,1,0:T(8,128)(2,1)}), bf16[3,512,512]{2,1,0:T(8,128)(2,1)}) %all-gather.3.cloned.1.call-update) | async-done | bytes 1572880 | tf_op jit(solution)/shard_map/all_gather | solution.py:50
  107.3 0.0 copy-done
  107.3 0.0 copy-done.5
  107.3 0.0 copy-done.6
  107.3 0.0 copy-start.1
  107.3 3.5 %divide_convert_fusion = (bf16[3,16,512]{2,1,0:T(8,128)(2,1)}, f32[3,16,512]{2,1,0:T(8,128)}, f32[3,16,512]{2,1,0:T(8,128)}) fusion(f32[3,16,512]{2,1,0:T(8,128)S(1)} %copy-done.5, f32[3,16,512]{2,1,0:T(8,128)S(1)} %copy-done.6, bf16[3,512,512]{2,1,0:T(8,128)(2,1)} %all-gather.3.cloned.1.call-done, bf16[3,512,512]{2,1,0:T(8,128)(2,1)S(1)} %copy-done, ...), kind=kOutput, calls=%fused_computation.24 | convolution fusion | flops 831504384 | bytes 3981316 | tf_op jit(solution)/shard_map/sji,sjk->sik/dot_general | solution.py:54
  110.8 0.0 all-gather.5.cloned.1.call-update
  110.8 0.0 copy-done.2
  110.8 0.0 copy-done.3
  110.9 0.0 copy-done.1
  110.9 1.2 fusion.8
  112.0 0.0 copy-start.4
  112.0 79.3 %all-gather.5.cloned.1.call-done = bf16[3,512,512]{2,1,0:T(8,128)(2,1)} async-done(((bf16[3,16,512]{2,1,0:T(8,128)(2,1)}), bf16[3,512,512]{2,1,0:T(8,128)(2,1)}) %all-gather.5.cloned.1.call-update) | async-done | bytes 1572880 | tf_op jit(solution)/shard_map/all_gather | solution.py:58
  191.3 2.6 fusion.10
  193.9 1.1 copy.45
  195.0 2.1 reshape.32
  197.1 0.0 copy-start.7
  197.1 7.6 %all-to-all-start.1 = ((bf16[16,2,768]{2,1,0:T(2,128)(2,1)}), bf16[16,2,768]{2,1,0:T(2,128)(2,1)S(1)}, u32[]{:S(2)}, u32[]{:S(2)}) async-start(bf16[16,2,768]{2,1,0:T(2,128)(2,1)} %reshape.32), calls=%async_computation.1 | async-start | bytes 98304 | tf_op jit(solution)/shard_map/all_to_all | solution.py:76
  204.8 0.0 copy-done.4
  204.8 1.2 fusion.7
  205.9 6.6 %all-to-all-done.1 = bf16[16,2,768]{2,1,0:T(2,128)(2,1)S(1)} async-done(((bf16[16,2,768]{2,1,0:T(2,128)(2,1)}), bf16[16,2,768]{2,1,0:T(2,128)(2,1)S(1)}, u32[]{:S(2)}, u32[]{:S(2)}) %all-to-all-start.1) | async-done | bytes 49184 | tf_op jit(solution)/shard_map/all_to_all | solution.py:76
  212.5 0.5 reshape.33
  213.0 0.2 copy.46
  213.2 0.0 copy-done.7
  213.2 0.2 fusion.6
  213.5 56.3 %all_gather.11 = bf16[24,512,32]{2,0,1:T(8,128)(2,1)} all-gather(bf16[24,16,32]{2,0,1:T(8,128)(2,1)S(1)} %fusion.6), channel_id=1, replica_groups=mesh['dp'=32,'tensor'=16] {'dp'}, dimensions={1}, use_global_device_ids=true | all-gather | bytes 811008 | tf_op jit(solution)/shard_map/all_gather | solution.py:85
  269.7 4.5 %copy.49 = bf16[24,512,32]{1,2,0:T(8,128)(2,1)} copy(bf16[24,512,32]{2,0,1:T(8,128)(2,1)} %all_gather.11) | data formatting | bytes 1572864
Async XLA Ops:
  7.2 100.1 %copy-start = (bf16[3,512,512]{2,1,0:T(8,128)(2,1)S(1)}, bf16[3,512,512]{2,1,0:T(8,128)(2,1)}, u32[]{:S(2)}) copy-start(bf16[3,512,512]{2,1,0:T(8,128)(2,1)} %param.13) | copy-start | bytes 4718596
  7.2 100.1 %copy-start.5 = (f32[3,16,512]{2,1,0:T(8,128)S(1)}, f32[3,16,512]{2,1,0:T(8,128)}, u32[]{:S(2)}) copy-start(f32[3,16,512]{2,1,0:T(8,128)} %param.17) | copy-start | bytes 294916
  7.2 100.1 %copy-start.6 = (f32[3,16,512]{2,1,0:T(8,128)S(1)}, f32[3,16,512]{2,1,0:T(8,128)}, u32[]{:S(2)}) copy-start(f32[3,16,512]{2,1,0:T(8,128)} %param.16) | copy-start | bytes 294916
  7.2 100.1 %all-gather.3.cloned.1.call-start = ((), (), s32[]{:S(2)}) async-start(), calls=%async_computation.2 | async-start | bytes 1622016 | tf_op jit(solution)/shard_map/all_gather | solution.py:50
  29.5 161.9 %all-gather.5.cloned.1.call-start = ((), (), s32[]{:S(2)}) async-start(), calls=%async_computation.3 | async-start | bytes 1622016 | tf_op jit(solution)/shard_map/all_gather | solution.py:58
  29.5 81.3 %copy-start.2 = (bf16[3,16,512]{2,1,0:T(8,128)(2,1)S(1)}, bf16[3,16,512]{2,1,0:T(8,128)(2,1)}, u32[]{:S(2)}) copy-start(bf16[3,16,512]{2,1,0:T(8,128)(2,1)} %squeeze.7) | copy-start | bytes 147460
  29.5 81.3 %copy-start.3 = (f32[3,16,512]{2,1,0:T(8,128)S(1)}, f32[3,16,512]{2,1,0:T(8,128)}, u32[]{:S(2)}) copy-start(f32[3,16,512]{2,1,0:T(8,128)} %param.14) | copy-start | bytes 294916
  107.3 3.6 %copy-start.1 = (bf16[3,512,512]{2,1,0:T(8,128)(2,1)S(1)}, bf16[3,512,512]{2,1,0:T(8,128)(2,1)}, u32[]{:S(2)}) copy-start(bf16[3,512,512]{2,1,0:T(8,128)(2,1)} %all-gather.3.cloned.1.call-done) | copy-start | bytes 4718596
  112.0 92.7 %copy-start.4 = (f32[3,16,512]{2,1,0:T(8,128)S(1)}, f32[3,16,512]{2,1,0:T(8,128)}, u32[]{:S(2)}) copy-start(f32[3,16,512]{2,1,0:T(8,128)} %param.15) | copy-start | bytes 294916
  197.1 16.1 %copy-start.7 = (bf16[24,16,32]{2,1,0:T(8,128)(2,1)S(1)}, bf16[24,16,32]{2,1,0:T(8,128)(2,1)}, u32[]{:S(2)}) copy-start(bf16[24,16,32]{2,1,0:T(8,128)(2,1)} %param.10) | copy-start | bytes 73732
  197.1 15.4 %all-to-all-start.1 = ((bf16[16,2,768]{2,1,0:T(2,128)(2,1)}), bf16[16,2,768]{2,1,0:T(2,128)(2,1)S(1)}, u32[]{:S(2)}, u32[]{:S(2)}) async-start(bf16[16,2,768]{2,1,0:T(2,128)(2,1)} %reshape.32), calls=%async_computation.1 | async-start | bytes 98304 | tf_op jit(solution)/shard_map/all_to_all | solution.py:76
Sparse Core Ops, SparseCore 0:
  29.6 77.6 all-gather.2
  111.0 80.2 all-gather.4
where the time goes:
time: 282 us; the launch traced here: 281 us
  waiting for transfers between devices  164 us (58%)
  blocking collectives  74.2 us (26%)
  between operations  14.2 us (5%)
  local copies, waits for them, and re-layouts  9.87 us (3%)
  matrix products  9.85 us (3%)
  starting transfers between devices  7.7 us (3%)
    all_gather x1, waiting for transfers between devices, per_device(): full_direction = lax.all_gather(direction, 'dp', axis=1, tiled=True)  79.3 us
    all_gather x1, waiting for transfers between devices, per_device(): full_grad = lax.all_gather(received, 'dp', axis=1, tiled=True)  77.8 us
    all_gather x1, blocking collectives, per_device(): new_weight = lax.all_gather(stepped, 'dp', axis=1, tiled=True)  56.3 us
    all_to_all x1, blocking collectives, per_device(): lax.all_to_all(packed, 'tensor', split_axis=0, concat_axis=3, tiled=True)[0]  18 us
    all_to_all x1, starting transfers between devices, per_device(): lax.all_to_all(update[None], 'tensor', split_axis=3, concat_axis=0, tiled...  7.62 us
    unnamed x21, local copies, waits for them, and re-layouts  7.47 us
    all_to_all x1, waiting for transfers between devices, per_device(): lax.all_to_all(update[None], 'tensor', split_axis=3, concat_axis=0, tiled...  6.55 us
  transfers between devices with their start and end apart: 3, of which 3 were waited for; matrix products, arithmetic and copies ran while one was open for 1% of the time, Pallas kernels for 0%

commit v1 on v0

v1 whole, which is shorter than its diff:
```python
import jax
import jax.numpy as jnp
from jax import lax
from jax.experimental import pallas as pl
from jax.experimental.pallas import tpu as pltpu
from jax.sharding import PartitionSpec as P

beta_one = 0.9
beta_two = 0.999
beta_gram = 0.95
epsilon = 1e-08
learn_rate = 0.01
decay_rate = 0.1

MESH = pl.DeviceIdType.MESH
F32 = jnp.float32
BF16 = jnp.bfloat16

NX = 4
NY = 8
ND = NX * NY
NT = 16
NB = 24
NS = 3
N = 512
R = 16
C = 32


def dot_nt(a, b):
    return lax.dot_general(a, b, (((1,), (1,)), ((), ())), preferred_element_type=F32)


def dot_nn(a, b):
    return lax.dot_general(a, b, (((1,), (0,)), ((), ())), preferred_element_type=F32)


def ring_gather(buf, ssem, rsem, x, y):
    count = [0]
    started = []

    def place(dx, dy):
        return lax.rem(x + dx + NX, NX) * NY + lax.rem(y + dy + NY, NY)

    def send(flow, dx, dy, tx, ty):
        src = place(dx, dy)
        copy = pltpu.make_async_remote_copy(
            src_ref=buf.at[flow, src],
            dst_ref=buf.at[flow, src],
            send_sem=ssem.at[count[0]],
            recv_sem=rsem.at[flow, src],
            device_id={"dp": place(tx, ty)},
            device_id_type=MESH,
        )
        count[0] += 1
        copy.start()
        started.append(copy)

    def arrive(flow, dx, dy):
        src = place(dx, dy)
        pltpu.make_async_remote_copy(
            src_ref=buf.at[flow, src],
            dst_ref=buf.at[flow, src],
            send_sem=ssem.at[0],
            recv_sem=rsem.at[flow, src],
            device_id={"dp": place(1, 0)},
            device_id_type=MESH,
        ).wait_recv()

    events = []

    def add(time, flow, dx, dy, forwards):
        events.append((time, len(events), flow, dx, dy, forwards))

    legs = [(0, 0)] + [(-k, k) for k in range(1, 5)] + [(k, k) for k in range(1, 4)]
    for dy, time in legs:
        forwards = []
        if -3 <= dy <= 0:
            forwards.append((0, 1))
        if 0 <= dy <= 2:
            forwards.append((0, -1))
        forwards += [(1, 0), (-1, 0)]
        add(time, 0, 0, dy, forwards)
        right = dy in (-4, -2, 1, 3)
        add(time + 1, 0, -1, dy, [(1, 0)] if right else [])
        add(time + 1, 0, 1, dy, [] if right else [(-1, 0)])
        add(time + 2, 0, 2, dy, [])
    for dx, first in ((0, 0), (1, 1), (-1, 1), (2, 1.5)):
        up, down = (4, 3) if dx in (0, 2) else (3, 4)
        forwards = [(0, 1), (0, -1)]
        if dx == 0:
            forwards = [(1, 0), (-1, 0), (2, 0)] + forwards
        add(first, 1, dx, 0, forwards)
        for k in range(1, up + 1):
            add(first + k, 1, dx, -k, [(0, 1)] if k < up else [])
        for k in range(1, down + 1):
            add(first + k, 1, dx, k, [(0, -1)] if k < down else [])

    for time, _, flow, dx, dy, forwards in sorted(events):
        if dx != 0 or dy != 0:
            arrive(flow, dx, dy)
        for tx, ty in forwards:
            send(flow, dx, dy, tx, ty)
    return started


def kernel(
    own,
    grad,
    weight,
    ql_hbm,
    qr_hbm,
    lg_hbm,
    rg_hbm,
    m1_hbm,
    m2_hbm,
    out_w,
    nl_hbm,
    nr_hbm,
    nm1_hbm,
    nm2_hbm,
    ql,
    qr,
    lg,
    rg,
    m1,
    m2,
    wide,
    wrow,
    zsend,
    zrecv,
    gbuf,
    qlc,
    dpad,
    bsend,
    brecv,
    vpad,
    usend,
    urecv,
    ysend,
    yrecv,
    wbuf,
    lsem,
    osem,
    zssem,
    zrsem,
    gssem,
    grsem,
    bssem,
    brsem,
    ussem,
    ursem,
    yssem,
    yrsem,
    wrsem,
):
    d = lax.axis_index("dp")
    t = lax.axis_index("tensor")
    x = d // NY
    y = lax.rem(d, NY)

    barrier = pltpu.get_barrier_semaphore()
    for k in range(1, NT):
        pl.semaphore_signal(
            barrier, inc=1, device_id={"tensor": lax.rem(t + k, NT)}, device_id_type=MESH
        )
    for k in range(1, ND):
        pl.semaphore_signal(
            barrier, inc=1, device_id={"dp": lax.rem(d + k, ND)}, device_id_type=MESH
        )

    loads = []
    for i, (src, dst) in enumerate(
        ((ql_hbm, ql), (qr_hbm, qr), (m1_hbm, m1), (m2_hbm, m2), (lg_hbm, lg), (rg_hbm, rg))
    ):
        copy = pltpu.make_async_copy(src, dst, lsem.at[i])
        copy.start()
        loads.append(copy)

    owner = [own[b] for b in range(NB)]
    position = []
    for b in range(NB):
        before = jnp.int32(0)
        for b2 in range(b):
            before = before + (owner[b2] == owner[b]).astype(jnp.int32)
        position.append(before)

    lane = lax.broadcasted_iota(jnp.int32, (C, 128), 1)
    row = lax.broadcasted_iota(jnp.int32, (C, 128), 0)
    repeat = jnp.where(lax.rem(lane, C) == row, 1.0, 0.0).astype(BF16)
    wide[...] = dot_nn(grad[...].reshape(NB * R, C), repeat)
    group32 = lax.broadcasted_iota(jnp.int32, (R, 128), 1) // 32
    group16 = lax.broadcasted_iota(jnp.int32, (R, 128), 1) // 16
    zero = jnp.zeros((R, 128), F32)

    u = lax.rem(t, 4)
    place = [lax.rem(u + position[b], 4) for b in range(NB)]
    for o in range(NT):
        tile = zero
        for b in range(NB):
            chosen = jnp.where(owner[b] == o, place[b], -1)
            tile = jnp.where(group32 == chosen, wide[b * R : (b + 1) * R, :], tile)
        zsend[o] = tile.astype(BF16)

    pl.semaphore_wait(barrier, NT - 1 + ND - 1)

    zcopies = []
    for k in range(1, NT):
        o = lax.rem(t + k, NT)
        copy = pltpu.make_async_remote_copy(
            src_ref=zsend.at[o],
            dst_ref=zrecv.at[t],
            send_sem=zssem.at[k],
            recv_sem=zrsem.at[t],
            device_id={"tensor": o},
            device_id_type=MESH,
        )
        copy.start()
        zcopies.append(copy)
    zrecv[t] = zsend[t]

    wwide = dot_nn(weight[...].reshape(NB * R, C), repeat)
    for k in range(NB // 4):
        tile = zero
        for j in range(4):
            b = 4 * k + j
            tile = jnp.where(group32 == j, wwide[b * R : (b + 1) * R, :], tile)
        wrow[:, 128 * k : 128 * (k + 1)] = tile
    for s in range(NS):
        dpad[s] = jnp.zeros((128, N), BF16)
        vpad[s] = jnp.zeros((128, N), BF16)

    for k in range(1, NT):
        o = lax.rem(t + k, NT)
        pltpu.make_async_remote_copy(
            src_ref=zsend.at[o],
            dst_ref=zrecv.at[o],
            send_sem=zssem.at[k],
            recv_sem=zrsem.at[o],
            device_id={"tensor": o},
            device_id_type=MESH,
        ).wait_recv()

    for k in range(4):
        tiles = [zrecv[4 * k + j].astype(F32) for j in range(4)]
        for s in range(NS):
            tile = zero
            for j in range(4):
                tile = jnp.where(group32 == (j + s) % 4, tiles[j], tile)
            if s:
                tile = pltpu.roll(tile, 128 - 32 * s, 1)
            gbuf[k // 2, d, s, :, 128 * (k % 2) : 128 * (k % 2 + 1)] = tile.astype(BF16)

    gcopies = ring_gather(gbuf, gssem, grsem, x, y)

    m = lax.rem(d, 8)
    tile_start = pl.multiple_of(128 * (d // 8), 128)
    pick = jnp.where(
        lax.broadcasted_iota(jnp.int32, (R, 128), 1)
        == lax.broadcasted_iota(jnp.int32, (R, 128), 0) + 16 * m,
        1.0,
        0.0,
    ).astype(BF16)
    loads[0].wait()
    for s in range(NS):
        qlc[s] = dot_nt(pick, ql[s, :, pl.ds(tile_start, 128)]).astype(BF16)

    def whole(flow, s):
        return gbuf[flow, :, s].reshape(N, N // 2)

    for i in range(1, 4):
        loads[i].wait()
    stores = []
    for s in range(NS):
        turned = jnp.concatenate([dot_nn(qlc[s], whole(f, s)) for f in range(2)], axis=1)
        high = turned.astype(BF16)
        low = (turned - high.astype(F32)).astype(BF16)
        both = dot_nn(jnp.concatenate([high, low], axis=0), qr[s])
        rotated = both[:R] + both[R:]
        first = beta_one * m1[s] + (1.0 - beta_one) * rotated
        second = beta_two * m2[s] + (1.0 - beta_two) * rotated * rotated
        m1[s] = first
        m2[s] = second
        direction = (first / (jnp.sqrt(second) + epsilon)).astype(BF16)
        at = pl.multiple_of(16 * lax.rem(m + s, 8), 16)
        dpad[s, pl.ds(at, 16), :] = direction
    for i, (src, dst) in enumerate(((m1, nm1_hbm), (m2, nm2_hbm))):
        copy = pltpu.make_async_copy(src, dst, osem.at[i])
        copy.start()
        stores.append(copy)

    turned = dot_nt(qr[0], dpad[0])
    for s in range(1, NS):
        turned = turned + dot_nt(qr[s], dpad[s])
    bsend[...] = turned.astype(BF16).reshape(ND, R, 128)

    def exchange(src, dst, ssem, rsem):
        copies = []
        for dx in (2, 1, 3, 0):
            for dy in (4, 3, 5, 2, 6, 1, 7, 0):
                if dx == 0 and dy == 0:
                    continue
                k = dx * NY + dy
                to = lax.rem(x + dx, NX) * NY + lax.rem(y + dy, NY)
                copy = pltpu.make_async_remote_copy(
                    src_ref=src.at[to],
                    dst_ref=dst.at[d],
                    send_sem=ssem.at[k],
                    recv_sem=rsem.at[d],
                    device_id={"dp": to},
                    device_id_type=MESH,
                )
                copy.start()
                copies.append(copy)
        dst[d] = src[d]
        return copies

    def received(src, dst, ssem, rsem):
        for k in range(1, ND):
            o = lax.rem(d + k, ND)
            pltpu.make_async_remote_copy(
                src_ref=src.at[o],
                dst_ref=dst.at[o],
                send_sem=ssem.at[k],
                recv_sem=rsem.at[o],
                device_id={"dp": o},
                device_id_type=MESH,
            ).wait_recv()

    bcopies = exchange(bsend, brecv, bssem, brsem)

    gram_scale = 1.0 - beta_gram
    loads[4].wait()
    for s in range(NS):
        mine = [gbuf[f, d, s] for f in range(2)]
        product = dot_nt(mine[0], whole(0, s)) + dot_nt(mine[1], whole(1, s))
        lg[s] = beta_gram * lg[s] + gram_scale * product
    copy = pltpu.make_async_copy(lg, nl_hbm, osem.at[2])
    copy.start()
    stores.append(copy)

    received(bsend, brecv, bssem, brsem)

    h = lax.rem(d, 2)
    for k in range(4):
        tiles = [brecv[8 * k + j].astype(F32) for j in range(8)]
        for s in range(NS):
            tile = zero
            for j in range(8):
                tile = jnp.where(group16 == (j + s) % 8, tiles[j], tile)
            if s:
                tile = pltpu.roll(tile, 128 - 16 * s, 1)
            at = pl.multiple_of(32 * s + 16 * h, 16)
            vpad[s, pl.ds(at, 16), 128 * k : 128 * (k + 1)] = tile.astype(BF16)
    update = dot_nt(ql[0], vpad[0])
    for s in range(1, NS):
        update = update + dot_nt(ql[s], vpad[s])
    usend[...] = update.astype(BF16).reshape(ND, R, 128)
    ucopies = exchange(usend, urecv, ussem, ursem)

    loads[5].wait()
    flow = d // 16
    within = pl.multiple_of(128 * lax.rem(d // 8, 2), 128)
    for s in range(NS):
        part = gbuf[flow, :, s, :, pl.ds(within, 128)].reshape(N, 128)
        columns = dot_nt(pick, part).astype(BF16)
        product = jnp.concatenate([dot_nn(columns, whole(f, s)) for f in range(2)], axis=1)
        rg[s] = beta_gram * rg[s] + gram_scale * product
    copy = pltpu.make_async_copy(rg, nr_hbm, osem.at[3])
    copy.start()
    stores.append(copy)

    received(usend, urecv, ussem, ursem)

    for o in range(NT):
        ysend[o] = (urecv[2 * o].astype(F32) + urecv[2 * o + 1].astype(F32)).astype(BF16)
    ycopies = []
    for k in range(1, NT):
        o = lax.rem(t + k, NT)
        copy = pltpu.make_async_remote_copy(
            src_ref=ysend.at[o],
            dst_ref=yrecv.at[t],
            send_sem=yssem.at[k],
            recv_sem=yrsem.at[t],
            device_id={"tensor": o},
            device_id_type=MESH,
        )
        copy.start()
        ycopies.append(copy)
    yrecv[t] = ysend[t]
    for copy in gcopies:
        copy.wait_send()
    for k in range(1, NT):
        o = lax.rem(t + k, NT)
        pltpu.make_async_remote_copy(
            src_ref=ysend.at[o],
            dst_ref=yrecv.at[o],
            send_sem=yssem.at[k],
            recv_sem=yrsem.at[o],
            device_id={"tensor": o},
            device_id_type=MESH,
        ).wait_recv()

    for k in range(NB // 4):
        tile = zero
        for j in range(4):
            b = 4 * k + j
            moved = pltpu.roll(
                yrecv[owner[b]].astype(F32), lax.rem(j - position[b] + 4, 4) * 32, 1
            )
            tile = jnp.where(group32 == j, moved, tile)
        old = wrow[:, 128 * k : 128 * (k + 1)]
        new = old - learn_rate * (tile + decay_rate * old)
        wbuf[k // 3, d, :, 128 * (k % 3) : 128 * (k % 3 + 1)] = new.astype(BF16)

    wcopies = ring_gather(wbuf, gssem, wrsem, x, y)

    eye = jnp.where(
        lax.broadcasted_iota(jnp.int32, (128, 128), 0)
        == lax.broadcasted_iota(jnp.int32, (128, 128), 1),
        1.0,
        0.0,
    ).astype(BF16)
    for k in range(NB // 4):
        part = wbuf[k // 3, :, :, 128 * (k % 3) : 128 * (k % 3 + 1)].reshape(N, 128)
        out_w[128 * k : 128 * (k + 1), :] = dot_nt(eye, part).astype(BF16)

    for copy in zcopies + bcopies + ucopies + ycopies + wcopies:
        copy.wait_send()
    for copy in stores:
        copy.wait()


def per_device(gradient, weight, owner_map, ql, qr, lg, rg, m1, m2):
    vmem = pl.BlockSpec(memory_space=pltpu.VMEM)
    anywhere = pl.BlockSpec(memory_space=pl.ANY)
    rows = jax.ShapeDtypeStruct((NS, R, N), F32)
    dma = pltpu.SemaphoreType.DMA
    outs = pl.pallas_call(
        kernel,
        out_shape=(jax.ShapeDtypeStruct((NB * C, N), BF16), rows, rows, rows, rows),
        in_specs=[pl.BlockSpec(memory_space=pltpu.SMEM), vmem, vmem] + [anywhere] * 6,
        out_specs=(vmem, anywhere, anywhere, anywhere, anywhere),
        scratch_shapes=[
            pltpu.VMEM((NS, N, N), BF16),
            pltpu.VMEM((NS, N, N), BF16),
            pltpu.VMEM((NS, R, N), F32),
            pltpu.VMEM((NS, R, N), F32),
            pltpu.VMEM((NS, R, N), F32),
            pltpu.VMEM((NS, R, N), F32),
            pltpu.VMEM((NB * R, 128), F32),
            pltpu.VMEM((R, NB * C), F32),
            pltpu.VMEM((NT, R, 128), BF16),
            pltpu.VMEM((NT, R, 128), BF16),
            pltpu.VMEM((2, ND, NS, R, N // 2), BF16),
            pltpu.VMEM((NS, R, N), BF16),
            pltpu.VMEM((NS, 128, N), BF16),
            pltpu.VMEM((ND, R, 128), BF16),
            pltpu.VMEM((ND, R, 128), BF16),
            pltpu.VMEM((NS, 128, N), BF16),
            pltpu.VMEM((ND, R, 128), BF16),
            pltpu.VMEM((ND, R, 128), BF16),
            pltpu.VMEM((NT, R, 128), BF16),
            pltpu.VMEM((NT, R, 128), BF16),
            pltpu.VMEM((2, ND, R, NB * C // 2), BF16),
            dma((6,)),
            dma((4,)),
            dma((NT,)),
            dma((NT,)),
            dma((62,)),
            dma((2, ND)),
            dma((ND,)),
            dma((ND,)),
            dma((ND,)),
            dma((ND,)),
            dma((NT,)),
            dma((NT,)),
            dma((2, ND)),
        ],
        compiler_params=pltpu.CompilerParams(
            collective_id=0, has_side_effects=True, vmem_limit_bytes=32 * 1024 * 1024
        ),
        name="soap_step",
    )(owner_map.reshape(NB), gradient, weight, ql, qr, lg, rg, m1, m2)
    new_weight = jnp.transpose(outs[0].reshape(NB, C, N), (0, 2, 1))
    return (new_weight,) + tuple(outs[1:])


def solution(mesh):
    in_specs = (
        P(None, "dp", "tensor"),
        P(None, "dp", "tensor"),
        P(),
        P("tensor", None, None),
        P("tensor", None, None),
        P("tensor", "dp", None),
        P("tensor", "dp", None),
        P("tensor", "dp", None),
        P("tensor", "dp", None),
    )
    out_specs = (
        P(None, None, "tensor"),
        P("tensor", "dp", None),
        P("tensor", "dp", None),
        P("tensor", "dp", None),
        P("tensor", "dp", None),
    )
    return jax.shard_map(
        per_device, mesh=mesh, in_specs=in_specs, out_specs=out_specs, check_vma=False
    )
```

time: 282 us -> 100 us (0.35)
  the two profiles are of different devices: /device:TPU:6 before, /device:TPU:8 now
where the time goes in v1:
time: 100 us
  Pallas kernels  87.1 us (87%)
  local copies, waits for them, and re-layouts  12.3 us (12%)
    pallas_call x1, Pallas kernels, per_device(): pl.pallas_call(kernel, out_shape=(jax.ShapeDtypeStruct((NB * C, N), BF16)...  87.1 us
    unnamed x23, local copies, waits for them, and re-layouts  12.3 us

profile of v1, /device:TPU:8, one launch (start us, length us, event | category | flops | bytes accessed | tf_op | source)
XLA Modules:
  0.0 100.0 jit_solution(11664790010130001831)
XLA Ops:
  0.6 0.0 copy-start
  0.6 1.4 %copy-done = bf16[3,512,512]{2,1,0:T(8,128)(2,1)S(1)} copy-done((bf16[3,512,512]{2,1,0:T(8,128)(2,1)S(1)}, bf16[3,512,512]{2,1,0:T(8,128)(2,1)}, u32[]{:S(2)}) %copy-start) | copy-done | bytes 1572888
  2.0 0.0 copy-start.1
  2.0 1.4 %copy-done.1 = bf16[3,512,512]{2,1,0:T(8,128)(2,1)S(1)} copy-done((bf16[3,512,512]{2,1,0:T(8,128)(2,1)S(1)}, bf16[3,512,512]{2,1,0:T(8,128)(2,1)}, u32[]{:S(2)}) %copy-start.1) | copy-done | bytes 1572888
  3.5 0.0 copy-start.2
  3.5 0.9 copy-done.2
  4.3 0.0 copy-start.3
  4.3 0.9 copy-done.3
  5.2 0.0 copy-start.4
  5.2 0.9 copy-done.4
  6.1 0.0 copy-start.5
  6.1 0.9 copy-done.5
  7.0 0.0 copy-start.6
  7.0 0.9 copy-done.6
  7.9 0.0 copy-start.7
  7.9 0.9 copy-done.7
  8.8 0.0 copy-start.8
  8.8 0.7 copy-done.8
  9.5 87.1 %soap_step.1 = (bf16[768,512]{1,0:T(8,128)(2,1)S(1)}, f32[3,16,512]{2,1,0:T(8,128)S(1)}, f32[3,16,512]{2,1,0:T(8,128)S(1)}, f32[3,16,512]{2,1,0:T(8,128)S(1)}, f32[3,16,512]{2,1,0:T(8,128)S(1)}) custom-call(s32[24]{0:T(128)S(1)} %bitcast.5, bf16[24,16,32]{2,1,0:T(8,128)(2,1)S(1)} %copy-done.2, bf16[24,16,32]{2,1,0:T(8,128)(2,1)S(1)} %copy-done.3, ...), custom_call_target="tpu_custom_call" | custom-call | tf_op jit(solution)/shard_map/soap_step/pallas_call | solution.py:439
  96.5 0.9 copy.19
  97.4 0.6 copy.20
  98.1 0.6 copy.21
  98.7 0.6 copy.22
  99.3 0.6 copy.23
Async XLA Ops:
  0.6 1.4 %copy-start = (bf16[3,512,512]{2,1,0:T(8,128)(2,1)S(1)}, bf16[3,512,512]{2,1,0:T(8,128)(2,1)}, u32[]{:S(2)}) copy-start(bf16[3,512,512]{2,1,0:T(8,128)(2,1)} %ql_hbm.1) | copy-start | bytes 4718596
  2.0 1.4 %copy-start.1 = (bf16[3,512,512]{2,1,0:T(8,128)(2,1)S(1)}, bf16[3,512,512]{2,1,0:T(8,128)(2,1)}, u32[]{:S(2)}) copy-start(bf16[3,512,512]{2,1,0:T(8,128)(2,1)} %qr_hbm.1) | copy-start | bytes 4718596
  3.5 0.9 copy-start.2
  4.3 0.9 copy-start.3
  5.2 0.9 copy-start.4
  6.1 0.9 copy-start.5
  7.0 0.9 copy-start.6
  7.9 0.9 copy-start.7
  8.8 0.7 copy-start.8

commit v2 on v1

v2 whole, which is shorter than its diff:
```python
import jax
import jax.numpy as jnp
from jax import lax
from jax.experimental import pallas as pl
from jax.experimental.pallas import tpu as pltpu
from jax.sharding import PartitionSpec as P

beta_one = 0.9
beta_two = 0.999
beta_gram = 0.95
epsilon = 1e-08
learn_rate = 0.01
decay_rate = 0.1

MESH = pl.DeviceIdType.MESH
F32 = jnp.float32
BF16 = jnp.bfloat16

NX = 4
NY = 8
ND = NX * NY
NT = 16
NB = 24
NS = 3
N = 512
R = 16
C = 32
VMEM_LIMIT = 56 * 1024 * 1024


def dot_nt(a, b):
    return lax.dot_general(a, b, (((1,), (1,)), ((), ())), preferred_element_type=F32)


def dot_nn(a, b):
    return lax.dot_general(a, b, (((1,), (0,)), ((), ())), preferred_element_type=F32)


class PlaneGather:
    legs = (1, -1, 2, -2, 3, -3, 4)

    def __init__(self, buf, ssem, rsem, x, y):
        self.buf, self.ssem, self.rsem, self.x, self.y = buf, ssem, rsem, x, y
        self.started = []

    def place(self, dx, dy):
        return lax.rem(self.x + dx + NX, NX) * NY + lax.rem(self.y + dy + NY, NY)

    def copy_of(self, dx, dy, tx, ty):
        src = self.place(dx, dy)
        return pltpu.make_async_remote_copy(
            src_ref=self.buf.at[src],
            dst_ref=self.buf.at[src],
            send_sem=self.ssem.at[len(self.started)],
            recv_sem=self.rsem.at[src],
            device_id={"dp": self.place(tx, ty)},
            device_id_type=MESH,
        )

    def send(self, dx, dy, tx, ty):
        copy = self.copy_of(dx, dy, tx, ty)
        copy.start()
        self.started.append(copy)

    def arrive(self, dx, dy):
        src = self.place(dx, dy)
        pltpu.make_async_remote_copy(
            src_ref=self.buf.at[src],
            dst_ref=self.buf.at[src],
            send_sem=self.ssem.at[0],
            recv_sem=self.rsem.at[src],
            device_id={"dp": self.place(1, 0)},
            device_id_type=MESH,
        ).wait_recv()

    def along_y(self):
        for dy in self.legs:
            self.send(0, 0, 0, dy)

    def along_x(self, i):
        dy = 0
        if i > 0:
            dy = -self.legs[i - 1]
            self.arrive(0, dy)
        self.send(0, dy, 1, 0)
        self.send(0, dy, -1, 0)

    def onward(self, i):
        dy = 0 if i == 0 else -self.legs[i - 1]
        self.arrive(-1, dy)
        self.arrive(1, dy)
        if i % 2 == 0:
            self.send(-1, dy, 1, 0)
        else:
            self.send(1, dy, -1, 0)

    def last(self):
        for dy in (0,) + tuple(-k for k in self.legs):
            self.arrive(2, dy)


def kernel(
    own,
    grad,
    weight,
    ql_hbm,
    qr_hbm,
    lg_hbm,
    rg_hbm,
    m1_hbm,
    m2_hbm,
    w_hbm,
    nl_hbm,
    nr_hbm,
    nm1_hbm,
    nm2_hbm,
    out_w,
    ql,
    qr,
    lg,
    rg,
    m1,
    m2,
    wide,
    wrow,
    zsend,
    zrecv,
    gbuf,
    tall,
    hsend,
    hrecv,
    rsend,
    rrecv,
    dpad,
    bsend,
    brecv,
    vpad,
    usend,
    urecv,
    ysend,
    yrecv,
    wbuf,
    lsem,
    osem,
    zssem,
    zrsem,
    gssem,
    grsem,
    hssem,
    hrsem,
    rssem,
    rrsem,
    bssem,
    brsem,
    ussem,
    ursem,
    yssem,
    yrsem,
    wssem,
    wrsem,
):
    d = lax.axis_index("dp")
    t = lax.axis_index("tensor")
    x = d // NY
    y = lax.rem(d, NY)

    barrier = pltpu.get_barrier_semaphore()
    for k in range(1, NT):
        pl.semaphore_signal(
            barrier, inc=1, device_id={"tensor": lax.rem(t + k, NT)}, device_id_type=MESH
        )
    for k in range(1, ND):
        pl.semaphore_signal(
            barrier, inc=1, device_id={"dp": lax.rem(d + k, ND)}, device_id_type=MESH
        )

    def exchange(src, dst, ssem, rsem):
        copies = []
        for dx in (2, 1, 3, 0):
            for dy in (4, 3, 5, 2, 6, 1, 7, 0):
                if dx == 0 and dy == 0:
                    continue
                k = dx * NY + dy
                to = lax.rem(x + dx, NX) * NY + lax.rem(y + dy, NY)
                copy = pltpu.make_async_remote_copy(
                    src_ref=src.at[to],
                    dst_ref=dst.at[d],
                    send_sem=ssem.at[k],
                    recv_sem=rsem.at[d],
                    device_id={"dp": to},
                    device_id_type=MESH,
                )
                copy.start()
                copies.append(copy)
        dst[d] = src[d]
        return copies

    def received(src, dst, ssem, rsem):
        for k in range(1, ND):
            o = lax.rem(d + k, ND)
            pltpu.make_async_remote_copy(
                src_ref=src.at[o],
                dst_ref=dst.at[o],
                send_sem=ssem.at[k],
                recv_sem=rsem.at[o],
                device_id={"dp": o},
                device_id_type=MESH,
            ).wait_recv()

    loads = []
    for i, (src, dst) in enumerate(
        ((ql_hbm, ql), (qr_hbm, qr), (m1_hbm, m1), (m2_hbm, m2), (lg_hbm, lg), (rg_hbm, rg))
    ):
        copy = pltpu.make_async_copy(src, dst, lsem.at[i])
        copy.start()
        loads.append(copy)

    owner = [own[b] for b in range(NB)]
    position = []
    for b in range(NB):
        before = jnp.int32(0)
        for b2 in range(b):
            before = before + (owner[b2] == owner[b]).astype(jnp.int32)
        position.append(before)

    lane = lax.broadcasted_iota(jnp.int32, (C, 128), 1)
    row = lax.broadcasted_iota(jnp.int32, (C, 128), 0)
    repeat = jnp.where(lax.rem(lane, C) == row, 1.0, 0.0).astype(BF16)
    wide[...] = dot_nn(grad[...].reshape(NB * R, C), repeat)
    group32 = lax.broadcasted_iota(jnp.int32, (R, 128), 1) // 32
    group16 = lax.broadcasted_iota(jnp.int32, (R, 128), 1) // 16
    zero = jnp.zeros((R, 128), F32)

    u = lax.rem(t, 4)
    place = [lax.rem(u + position[b], 4) for b in range(NB)]
    for o in range(NT):
        tile = zero
        for b in range(NB):
            chosen = jnp.where(owner[b] == o, place[b], -1)
            tile = jnp.where(group32 == chosen, wide[b * R : (b + 1) * R, :], tile)
        zsend[o] = tile.astype(BF16)

    pl.semaphore_wait(barrier, NT - 1 + ND - 1)

    zcopies = []
    for k in range(1, NT):
        o = lax.rem(t + k, NT)
        copy = pltpu.make_async_remote_copy(
            src_ref=zsend.at[o],
            dst_ref=zrecv.at[t],
            send_sem=zssem.at[k],
            recv_sem=zrsem.at[t],
            device_id={"tensor": o},
            device_id_type=MESH,
        )
        copy.start()
        zcopies.append(copy)
    zrecv[t] = zsend[t]

    wwide = dot_nn(weight[...].reshape(NB * R, C), repeat)
    for k in range(NB // 4):
        tile = zero
        for j in range(4):
            b = 4 * k + j
            tile = jnp.where(group32 == j, wwide[b * R : (b + 1) * R, :], tile)
        wrow[:, 128 * k : 128 * (k + 1)] = tile
    tall[...] = jnp.zeros((128, N), F32)
    for s in range(NS):
        dpad[s] = jnp.zeros((128, N), BF16)
        vpad[s] = jnp.zeros((128, N), BF16)

    for k in range(1, NT):
        o = lax.rem(t + k, NT)
        pltpu.make_async_remote_copy(
            src_ref=zsend.at[o],
            dst_ref=zrecv.at[o],
            send_sem=zssem.at[k],
            recv_sem=zrsem.at[o],
            device_id={"tensor": o},
            device_id_type=MESH,
        ).wait_recv()

    for k in range(4):
        tiles = [zrecv[4 * k + j].astype(F32) for j in range(4)]
        for s in range(NS):
            tile = zero
            for j in range(4):
                tile = jnp.where(group32 == (j + s) % 4, tiles[j], tile)
            if s:
                tile = pltpu.roll(tile, 128 - 32 * s, 1)
            gbuf[d, s, :, 128 * k : 128 * (k + 1)] = tile.astype(BF16)

    gather = PlaneGather(gbuf, gssem, grsem, x, y)
    m = lax.rem(d, 8)
    h = lax.rem(d, 2)

    def lane_groups(src, offset):
        parts = []
        for k in range(4):
            tile = zero
            for j in range(8):
                tile = jnp.where(group16 == (j + offset) % 8, src[8 * k + j].astype(F32), tile)
            if offset:
                tile = pltpu.roll(tile, 128 - 16 * offset, 1)
            parts.append(tile)
        return jnp.concatenate(parts, axis=1)

    def group_at(offset):
        return pl.ds(pl.multiple_of(16 * lax.rem(m + offset, 8), 16), 16)

    loads[1].wait()
    for s in range(NS):
        tall[group_at(s), :] = dot_nn(gbuf[d, s], qr[s])
    hsend[...] = tall[...].T.astype(BF16).reshape(ND, R, 128)
    hcopies = exchange(hsend, hrecv, hssem, hrsem)
    gather.along_y()

    loads[0].wait()
    received(hsend, hrecv, hssem, hrsem)
    for s in range(NS):
        half = lane_groups(hrecv, s).astype(BF16)
        turned = dot_nn(half, ql[s])
        high = turned.astype(BF16).astype(F32)
        tall[group_at(s), :] = high
        tall[group_at(s + 3), :] = turned - high
    rsend[...] = tall[...].T.astype(BF16).reshape(ND, R, 128)
    rcopies = exchange(rsend, rrecv, rssem, rrsem)
    for i in range(4):
        gather.along_x(i)

    for i in range(2, 4):
        loads[i].wait()
    received(rsend, rrecv, rssem, rrsem)
    stores = []
    for s in range(NS):
        rotated = lane_groups(rrecv, s) + lane_groups(rrecv, s + 3)
        first = beta_one * m1[s] + (1.0 - beta_one) * rotated
        second = beta_two * m2[s] + (1.0 - beta_two) * rotated * rotated
        m1[s] = first
        m2[s] = second
        direction = (first / (jnp.sqrt(second) + epsilon)).astype(BF16)
        dpad[s, group_at(s), :] = direction
    for i, (src, dst) in enumerate(((m1, nm1_hbm), (m2, nm2_hbm))):
        copy = pltpu.make_async_copy(src, dst, osem.at[i])
        copy.start()
        stores.append(copy)

    turned = dot_nt(qr[0], dpad[0])
    for s in range(1, NS):
        turned = turned + dot_nt(qr[s], dpad[s])
    bsend[...] = turned.astype(BF16).reshape(ND, R, 128)

    bcopies = exchange(bsend, brecv, bssem, brsem)

    for i in range(4, 8):
        gather.along_x(i)

    received(bsend, brecv, bssem, brsem)

    for s in range(NS):
        at = pl.multiple_of(32 * s + 16 * h, 16)
        vpad[s, pl.ds(at, 16), :] = lane_groups(brecv, s).astype(BF16)
    update = dot_nt(ql[0], vpad[0])
    for s in range(1, NS):
        update = update + dot_nt(ql[s], vpad[s])
    usend[...] = update.astype(BF16).reshape(ND, R, 128)
    ucopies = exchange(usend, urecv, ussem, ursem)

    for i in range(8):
        gather.onward(i)

    received(usend, urecv, ussem, ursem)

    for o in range(NT):
        ysend[o] = (urecv[2 * o].astype(F32) + urecv[2 * o + 1].astype(F32)).astype(BF16)
    ycopies = []
    for k in range(1, NT):
        o = lax.rem(t + k, NT)
        copy = pltpu.make_async_remote_copy(
            src_ref=ysend.at[o],
            dst_ref=yrecv.at[t],
            send_sem=yssem.at[k],
            recv_sem=yrsem.at[t],
            device_id={"tensor": o},
            device_id_type=MESH,
        )
        copy.start()
        ycopies.append(copy)
    yrecv[t] = ysend[t]
    for k in range(1, NT):
        o = lax.rem(t + k, NT)
        pltpu.make_async_remote_copy(
            src_ref=ysend.at[o],
            dst_ref=yrecv.at[o],
            send_sem=yssem.at[k],
            recv_sem=yrsem.at[o],
            device_id={"tensor": o},
            device_id_type=MESH,
        ).wait_recv()

    for k in range(NB // 4):
        tile = zero
        for j in range(4):
            b = 4 * k + j
            moved = pltpu.roll(
                yrecv[owner[b]].astype(F32), lax.rem(j - position[b] + 4, 4) * 32, 1
            )
            tile = jnp.where(group32 == j, moved, tile)
        old = wrow[:, 128 * k : 128 * (k + 1)]
        new = old - learn_rate * (tile + decay_rate * old)
        wbuf[d, :, 128 * k : 128 * (k + 1)] = new.astype(BF16)

    eye = jnp.where(
        lax.broadcasted_iota(jnp.int32, (128, 128), 0)
        == lax.broadcasted_iota(jnp.int32, (128, 128), 1),
        1.0,
        0.0,
    ).astype(BF16)
    final = PlaneGather(wbuf, wssem, wrsem, x, y)
    final.along_x(0)
    final.along_y()

    def whole(s):
        return gbuf[:, s].reshape(N, N)

    gather.last()
    gram_scale = 1.0 - beta_gram
    loads[4].wait()
    for s in range(NS):
        product = dot_nt(gbuf[d, s], whole(s))
        lg[s] = beta_gram * lg[s] + gram_scale * product
    copy = pltpu.make_async_copy(lg, nl_hbm, osem.at[2])
    copy.start()
    stores.append(copy)

    for i in range(1, 8):
        final.along_x(i)
        if i > 1:
            final.onward(i - 2)
    final.onward(6)
    final.onward(7)

    pick = jnp.where(
        lax.broadcasted_iota(jnp.int32, (R, 128), 1)
        == lax.broadcasted_iota(jnp.int32, (R, 128), 0) + 16 * m,
        1.0,
        0.0,
    ).astype(BF16)
    tile_start = pl.multiple_of(128 * (d // 8), 128)
    loads[5].wait()
    for s in range(NS):
        part = gbuf[:, s, :, pl.ds(tile_start, 128)].reshape(N, 128)
        columns = dot_nt(pick, part).astype(BF16)
        product = dot_nn(columns, whole(s))
        rg[s] = beta_gram * rg[s] + gram_scale * product
    copy = pltpu.make_async_copy(rg, nr_hbm, osem.at[3])
    copy.start()
    stores.append(copy)

    for dx in (0, 1, 3, 2):
        group = lax.rem(x + dx, NX)
        if dx == 2:
            final.last()
        rows = pl.ds(pl.multiple_of(NY * group, NY), NY)
        columns = pl.ds(pl.multiple_of(128 * group, 128), 128)
        for k in range(NB // 4):
            part = wbuf[rows, :, 128 * k : 128 * (k + 1)].reshape(128, 128)
            out_w[128 * k : 128 * (k + 1), columns] = dot_nt(eye, part).astype(BF16)
        copy = pltpu.make_async_copy(out_w.at[:, columns], w_hbm.at[:, columns], osem.at[4 + dx])
        copy.start()
        stores.append(copy)

    for copy in zcopies + hcopies + rcopies + bcopies + ucopies + ycopies:
        copy.wait_send()
    for copy in gather.started + final.started:
        copy.wait_send()
    for copy in stores:
        copy.wait()


def hand_over(
    w, nl, nr, nm1, nm2, w_out, nl_out, nr_out, nm1_out, nm2_out, w_v, nl_v, nr_v, nm1_v, nm2_v, sem
):
    triples = []
    for k in range(4):
        part = pl.ds(NB * C // 4 * k, NB * C // 4)
        triples.append((w.at[part], w_v.at[part], w_out.at[part]))
    triples += [(nl, nl_v, nl_out), (nr, nr_v, nr_out), (nm1, nm1_v, nm1_out), (nm2, nm2_v, nm2_out)]
    reads = [pltpu.make_async_copy(a, b, sem.at[0, i]) for i, (a, b, _) in enumerate(triples)]
    writes = [pltpu.make_async_copy(b, c, sem.at[1, i]) for i, (_, b, c) in enumerate(triples)]
    for copy in reads:
        copy.start()
    for read, write in zip(reads, writes):
        read.wait()
        write.start()
    for copy in writes:
        copy.wait()


def per_device(gradient, weight, owner_map, ql, qr, lg, rg, m1, m2):
    vmem = pl.BlockSpec(memory_space=pltpu.VMEM)
    anywhere = pl.BlockSpec(memory_space=pl.ANY)
    rows = jax.ShapeDtypeStruct((NS, R, N), F32)
    dma = pltpu.SemaphoreType.DMA
    outs = pl.pallas_call(
        kernel,
        out_shape=(jax.ShapeDtypeStruct((NB * C, N), BF16), rows, rows, rows, rows),
        in_specs=[pl.BlockSpec(memory_space=pltpu.SMEM), vmem, vmem] + [anywhere] * 6,
        out_specs=(anywhere,) * 5,
        scratch_shapes=[
            pltpu.VMEM((NB * C, N), BF16),
            pltpu.VMEM((NS, N, N), BF16),
            pltpu.VMEM((NS, N, N), BF16),
            pltpu.VMEM((NS, R, N), F32),
            pltpu.VMEM((NS, R, N), F32),
            pltpu.VMEM((NS, R, N), F32),
            pltpu.VMEM((NS, R, N), F32),
            pltpu.VMEM((NB * R, 128), F32),
            pltpu.VMEM((R, NB * C), F32),
            pltpu.VMEM((NT, R, 128), BF16),
            pltpu.VMEM((NT, R, 128), BF16),
            pltpu.VMEM((ND, NS, R, N), BF16),
            pltpu.VMEM((128, N), F32),
            pltpu.VMEM((ND, R, 128), BF16),
            pltpu.VMEM((ND, R, 128), BF16),
            pltpu.VMEM((ND, R, 128), BF16),
            pltpu.VMEM((ND, R, 128), BF16),
            pltpu.VMEM((NS, 128, N), BF16),
            pltpu.VMEM((ND, R, 128), BF16),
            pltpu.VMEM((ND, R, 128), BF16),
            pltpu.VMEM((NS, 128, N), BF16),
            pltpu.VMEM((ND, R, 128), BF16),
            pltpu.VMEM((ND, R, 128), BF16),
            pltpu.VMEM((NT, R, 128), BF16),
            pltpu.VMEM((NT, R, 128), BF16),
            pltpu.VMEM((ND, R, NB * C), BF16),
            dma((6,)),
            dma((8,)),
            dma((NT,)),
            dma((NT,)),
            dma((31,)),
            dma((ND,)),
            dma((ND,)),
            dma((ND,)),
            dma((ND,)),
            dma((ND,)),
            dma((ND,)),
            dma((ND,)),
            dma((ND,)),
            dma((ND,)),
            dma((NT,)),
            dma((NT,)),
            dma((31,)),
            dma((ND,)),
        ],
        compiler_params=pltpu.CompilerParams(
            collective_id=0, has_side_effects=True, vmem_limit_bytes=VMEM_LIMIT
        ),
        name="soap_step",
    )(owner_map.reshape(NB), gradient, weight, ql, qr, lg, rg, m1, m2)
    outs = pl.pallas_call(
        hand_over,
        out_shape=(jax.ShapeDtypeStruct((NB * C, N), BF16), rows, rows, rows, rows),
        in_specs=[anywhere] * 5,
        out_specs=(anywhere,) * 5,
        scratch_shapes=[pltpu.VMEM((NB * C, N), BF16)]
        + [pltpu.VMEM((NS, R, N), F32)] * 4
        + [dma((2, 8))],
        compiler_params=pltpu.CompilerParams(vmem_limit_bytes=VMEM_LIMIT),
        name="hand_over",
    )(*outs)
    new_weight = jnp.transpose(outs[0].reshape(NB, C, N), (0, 2, 1))
    return (new_weight,) + tuple(outs[1:])


def solution(mesh):
    in_specs = (
        P(None, "dp", "tensor"),
        P(None, "dp", "tensor"),
        P(),
        P("tensor", None, None),
        P("tensor", None, None),
        P("tensor", "dp", None),
        P("tensor", "dp", None),
        P("tensor", "dp", None),
        P("tensor", "dp", None),
    )
    out_specs = (
        P(None, None, "tensor"),
        P("tensor", "dp", None),
        P("tensor", "dp", None),
        P("tensor", "dp", None),
        P("tensor", "dp", None),
    )
    return jax.shard_map(
        per_device, mesh=mesh, in_specs=in_specs, out_specs=out_specs, check_vma=False
    )
```

time: 100 us -> 84.5 us (0.84)
  the two profiles are of different devices: /device:TPU:8 before, /device:TPU:6 now
where the time goes in v2:
time: 84.5 us; the launch traced here: 84.3 us
  Pallas kernels  83.7 us (99%)
    pallas_call x1, Pallas kernels, per_device(): pl.pallas_call(kernel, out_shape=(jax.ShapeDtypeStruct((NB * C, N), BF16)...  81.5 us
    pallas_call x1, Pallas kernels, per_device(): pl.pallas_call(hand_over, out_shape=(jax.ShapeDtypeStruct((NB * C, N), BF...  2.16 us

profile of v2, /device:TPU:6, one launch (start us, length us, event | category | flops | bytes accessed | tf_op | source)
XLA Modules:
  0.0 84.3 jit_solution(16879817206175582380)
XLA Ops:
  0.6 81.5 %soap_step.1 = (bf16[768,512]{1,0:T(8,128)(2,1)}, f32[3,16,512]{2,1,0:T(8,128)}, f32[3,16,512]{2,1,0:T(8,128)}, f32[3,16,512]{2,1,0:T(8,128)}, f32[3,16,512]{2,1,0:T(8,128)}) custom-call(s32[24]{0:T(128)} %bitcast.4, bf16[24,16,32]{2,1,0:T(8,128)(2,1)} %grad.1, bf16[24,16,32]{2,1,0:T(8,128)(2,1)} %weight.1, bf16[3,512,512]{2,1,0:T(8,128)(2,1)} %ql_hbm.1, ...), custom_call_target="tpu_custom_call" | custom-call | tf_op jit(solution)/shard_map/soap_step/pallas_call | solution.py:505
  82.2 2.2 %hand_over.1 = (bf16[768,512]{1,0:T(8,128)(2,1)}, f32[3,16,512]{2,1,0:T(8,128)}, f32[3,16,512]{2,1,0:T(8,128)}, f32[3,16,512]{2,1,0:T(8,128)}, f32[3,16,512]{2,1,0:T(8,128)}) custom-call(bf16[768,512]{1,0:T(8,128)(2,1)} %get-tuple-element.15.w, f32[3,16,512]{2,1,0:T(8,128)} %get-tuple-element.16.nl, f32[3,16,512]{2,1,0:T(8,128)} %get-tuple-element.17.nr, ...), custom_call_target="tpu_custom_call" | custom-call | tf_op jit(solution)/shard_map/hand_over/pallas_call | solution.py:561

commit v3 on v2

--- a/solution.py
+++ b/solution.py
@@ -137,8 +137,6 @@
     vpad,
     usend,
     urecv,
-    ysend,
-    yrecv,
     wbuf,
     lsem,
     osem,
@@ -154,8 +152,6 @@
     brsem,
     ussem,
     ursem,
-    yssem,
-    yrsem,
     wssem,
     wrsem,
 ):
@@ -207,6 +203,18 @@
                 device_id_type=MESH,
             ).wait_recv()
 
+    target = d // 2
+    slot = 2 * t + lax.rem(d, 2)
+    apart = target != t
+    for i in range(ND):
+        at = 2 * t + i % 2
+
+        @pl.when(jnp.logical_or(apart, i != slot))
+        def _():
+            pl.semaphore_signal(
+                barrier, inc=1, device_id={"dp": at, "tensor": i // 2}, device_id_type=MESH
+            )
+
     loads = []
     for i, (src, dst) in enumerate(
         ((ql_hbm, ql), (qr_hbm, qr), (m1_hbm, m1), (m2_hbm, m2), (lg_hbm, lg), (rg_hbm, rg))
@@ -240,7 +248,7 @@
             tile = jnp.where(group32 == chosen, wide[b * R : (b + 1) * R, :], tile)
         zsend[o] = tile.astype(BF16)
 
-    pl.semaphore_wait(barrier, NT - 1 + ND - 1)
+    pl.semaphore_wait(barrier, NT - 1 + ND - 1 + ND - 1 + apart.astype(jnp.int32))
 
     zcopies = []
     for k in range(1, NT):
@@ -314,6 +322,7 @@
     hsend[...] = tall[...].T.astype(BF16).reshape(ND, R, 128)
     hcopies = exchange(hsend, hrecv, hssem, hrsem)
     gather.along_y()
+    gather.along_x(0)
 
     loads[0].wait()
     received(hsend, hrecv, hssem, hrsem)
@@ -325,7 +334,7 @@
         tall[group_at(s + 3), :] = turned - high
     rsend[...] = tall[...].T.astype(BF16).reshape(ND, R, 128)
     rcopies = exchange(rsend, rrecv, rssem, rrsem)
-    for i in range(4):
+    for i in range(1, 5):
         gather.along_x(i)
 
     for i in range(2, 4):
@@ -352,8 +361,10 @@
 
     bcopies = exchange(bsend, brecv, bssem, brsem)
 
-    for i in range(4, 8):
+    for i in range(5, 8):
         gather.along_x(i)
+    for i in range(8):
+        gather.onward(i)
 
     received(bsend, brecv, bssem, brsem)
 
@@ -364,47 +375,66 @@
     for s in range(1, NS):
         update = update + dot_nt(ql[s], vpad[s])
     usend[...] = update.astype(BF16).reshape(ND, R, 128)
-    ucopies = exchange(usend, urecv, ussem, ursem)
-
-    for i in range(8):
-        gather.onward(i)
-
-    received(usend, urecv, ussem, ursem)
-
-    for o in range(NT):
-        ysend[o] = (urecv[2 * o].astype(F32) + urecv[2 * o + 1].astype(F32)).astype(BF16)
-    ycopies = []
-    for k in range(1, NT):
-        o = lax.rem(t + k, NT)
-        copy = pltpu.make_async_remote_copy(
-            src_ref=ysend.at[o],
-            dst_ref=yrecv.at[t],
-            send_sem=yssem.at[k],
-            recv_sem=yrsem.at[t],
-            device_id={"tensor": o},
+
+    def update_copy(dx, dy):
+        to = lax.rem(x + dx, NX) * NY + lax.rem(y + dy, NY)
+        return pltpu.make_async_remote_copy(
+            src_ref=usend.at[to],
+            dst_ref=urecv.at[slot],
+            send_sem=ussem.at[dx * NY + dy],
+            recv_sem=ursem.at[slot],
+            device_id={"dp": to, "tensor": target},
             device_id_type=MESH,
         )
-        copy.start()
-        ycopies.append(copy)
-    yrecv[t] = ysend[t]
-    for k in range(1, NT):
-        o = lax.rem(t + k, NT)
-        pltpu.make_async_remote_copy(
-            src_ref=ysend.at[o],
-            dst_ref=yrecv.at[o],
-            send_sem=yssem.at[k],
-            recv_sem=yrsem.at[o],
-            device_id={"tensor": o},
-            device_id_type=MESH,
-        ).wait_recv()
+
+    ucopies = []
+    for dx in (2, 1, 3, 0):
+        for dy in (4, 3, 5, 2, 6, 1, 7, 0):
+            if dx or dy:
+                copy = update_copy(dx, dy)
+                copy.start()
+                ucopies.append(copy)
+
+    @pl.when(apart)
+    def _():
+        update_copy(0, 0).start()
+
+    @pl.when(jnp.logical_not(apart))
+    def _():
+        urecv[slot] = usend[d]
+
+    def whole(s):
+        return gbuf[:, s].reshape(N, N)
+
+    gather.last()
+    gram_scale = 1.0 - beta_gram
+    loads[4].wait()
+    for s in range(NS):
+        product = dot_nt(gbuf[d, s], whole(s))
+        lg[s] = beta_gram * lg[s] + gram_scale * product
+    copy = pltpu.make_async_copy(lg, nl_hbm, osem.at[2])
+    copy.start()
+    stores.append(copy)
+
+    for i in range(ND):
+
+        @pl.when(jnp.logical_or(apart, i != slot))
+        def _():
+            pltpu.make_async_remote_copy(
+                src_ref=usend.at[0],
+                dst_ref=urecv.at[i],
+                send_sem=ussem.at[0],
+                recv_sem=ursem.at[i],
+                device_id={"dp": 2 * t + i % 2, "tensor": i // 2},
+                device_id_type=MESH,
+            ).wait_recv()
 
     for k in range(NB // 4):
         tile = zero
         for j in range(4):
             b = 4 * k + j
-            moved = pltpu.roll(
-                yrecv[owner[b]].astype(F32), lax.rem(j - position[b] + 4, 4) * 32, 1
-            )
+            pair = urecv[2 * owner[b]].astype(F32) + urecv[2 * owner[b] + 1].astype(F32)
+            moved = pltpu.roll(pair, lax.rem(j - position[b] + 4, 4) * 32, 1)
             tile = jnp.where(group32 == j, moved, tile)
         old = wrow[:, 128 * k : 128 * (k + 1)]
         new = old - learn_rate * (tile + decay_rate * old)
@@ -419,19 +449,6 @@
     final = PlaneGather(wbuf, wssem, wrsem, x, y)
     final.along_x(0)
     final.along_y()
-
-    def whole(s):
-        return gbuf[:, s].reshape(N, N)
-
-    gather.last()
-    gram_scale = 1.0 - beta_gram
-    loads[4].wait()
-    for s in range(NS):
-        product = dot_nt(gbuf[d, s], whole(s))
-        lg[s] = beta_gram * lg[s] + gram_scale * product
-    copy = pltpu.make_async_copy(lg, nl_hbm, osem.at[2])
-    copy.start()
-    stores.append(copy)
 
     for i in range(1, 8):
         final.along_x(i)
@@ -470,10 +487,15 @@
         copy.start()
         stores.append(copy)
 
-    for copy in zcopies + hcopies + rcopies + bcopies + ucopies + ycopies:
+    for copy in zcopies + hcopies + rcopies + bcopies + ucopies:
         copy.wait_send()
     for copy in gather.started + final.started:
         copy.wait_send()
+
+    @pl.when(apart)
+    def _():
+        update_copy(0, 0).wait_send()
+
     for copy in stores:
         copy.wait()
 
@@ -531,8 +553,6 @@
             pltpu.VMEM((NS, 128, N), BF16),
             pltpu.VMEM((ND, R, 128), BF16),
             pltpu.VMEM((ND, R, 128), BF16),
-            pltpu.VMEM((NT, R, 128), BF16),
-            pltpu.VMEM((NT, R, 128), BF16),
             pltpu.VMEM((ND, R, NB * C), BF16),
             dma((6,)),
             dma((8,)),
@@ -548,8 +568,6 @@
             dma((ND,)),
             dma((ND,)),
             dma((ND,)),
-            dma((NT,)),
-            dma((NT,)),
             dma((31,)),
             dma((ND,)),
         ],

time: 84.5 us -> 86.3 us (1.021)
  Pallas kernels: 83.7 us -> 85.5 us
    pallas_call x1, Pallas kernels: 81.5 us -> 83.3 us  [per_device(): pl.pallas_call(kernel, out_shape=(jax.ShapeDtypeStruct((NB * C, N), BF16)...]
where the time goes in v3:
time: 86.3 us; the launch traced here: 86.1 us
  Pallas kernels  85.5 us (99%)
    pallas_call x1, Pallas kernels, per_device(): pl.pallas_call(kernel, out_shape=(jax.ShapeDtypeStruct((NB * C, N), BF16)...  83.3 us
    pallas_call x1, Pallas kernels, per_device(): pl.pallas_call(hand_over, out_shape=(jax.ShapeDtypeStruct((NB * C, N), BF...  2.16 us

profile of v3, /device:TPU:6, one launch (start us, length us, event | category | flops | bytes accessed | tf_op | source)
XLA Modules:
  0.0 86.1 jit_solution(18309222607214076872)
XLA Ops:
  0.6 83.3 %soap_step.1 = (bf16[768,512]{1,0:T(8,128)(2,1)}, f32[3,16,512]{2,1,0:T(8,128)}, f32[3,16,512]{2,1,0:T(8,128)}, f32[3,16,512]{2,1,0:T(8,128)}, f32[3,16,512]{2,1,0:T(8,128)}) custom-call(s32[24]{0:T(128)} %bitcast.4, bf16[24,16,32]{2,1,0:T(8,128)(2,1)} %grad.1, bf16[24,16,32]{2,1,0:T(8,128)(2,1)} %weight.1, bf16[3,512,512]{2,1,0:T(8,128)(2,1)} %ql_hbm.1, ...), custom_call_target="tpu_custom_call" | custom-call | tf_op jit(solution)/shard_map/soap_step/pallas_call | solution.py:527
  84.0 2.2 %hand_over.1 = (bf16[768,512]{1,0:T(8,128)(2,1)}, f32[3,16,512]{2,1,0:T(8,128)}, f32[3,16,512]{2,1,0:T(8,128)}, f32[3,16,512]{2,1,0:T(8,128)}, f32[3,16,512]{2,1,0:T(8,128)}) custom-call(bf16[768,512]{1,0:T(8,128)(2,1)} %get-tuple-element.15.w, f32[3,16,512]{2,1,0:T(8,128)} %get-tuple-element.16.nl, f32[3,16,512]{2,1,0:T(8,128)} %get-tuple-element.17.nr, ...), custom_call_target="tpu_custom_call" | custom-call | tf_op jit(solution)/shard_map/hand_over/pallas_call | solution.py:579

commit v4 on v2

--- a/solution.py
+++ b/solution.py
@@ -51,7 +51,7 @@
         return pltpu.make_async_remote_copy(
             src_ref=self.buf.at[src],
             dst_ref=self.buf.at[src],
-            send_sem=self.ssem.at[len(self.started)],
+            send_sem=self.ssem.at[0],
             recv_sem=self.rsem.at[src],
             device_id={"dp": self.place(tx, ty)},
             device_id_type=MESH,
@@ -77,6 +77,19 @@
         for dy in self.legs:
             self.send(0, 0, 0, dy)
 
+    def begin(self):
+        for tx, ty in ((0, 1), (0, -1), (1, 0), (-1, 0)):
+            self.send(0, 0, tx, ty)
+
+    def ring(self, k):
+        for dy, ty, end in ((-k, 1, 4), (k, -1, 3)):
+            if k <= end:
+                self.arrive(0, dy)
+                if k < end:
+                    self.send(0, dy, 0, ty)
+                self.send(0, dy, 1, 0)
+                self.send(0, dy, -1, 0)
+
     def along_x(self, i):
         dy = 0
         if i > 0:
@@ -93,6 +106,17 @@
             self.send(-1, dy, 1, 0)
         else:
             self.send(1, dy, -1, 0)
+
+    def finish(self):
+        chunks = self.buf.at[pl.ds(0, len(self.started))]
+        pltpu.make_async_remote_copy(
+            src_ref=chunks,
+            dst_ref=chunks,
+            send_sem=self.ssem.at[0],
+            recv_sem=self.rsem.at[0],
+            device_id={"dp": self.place(1, 0)},
+            device_id_type=MESH,
+        ).wait_send()
 
     def last(self):
         for dy in (0,) + tuple(-k for k in self.legs):
@@ -175,37 +199,34 @@
         )
 
     def exchange(src, dst, ssem, rsem):
-        copies = []
         for dx in (2, 1, 3, 0):
             for dy in (4, 3, 5, 2, 6, 1, 7, 0):
                 if dx == 0 and dy == 0:
                     continue
-                k = dx * NY + dy
                 to = lax.rem(x + dx, NX) * NY + lax.rem(y + dy, NY)
                 copy = pltpu.make_async_remote_copy(
                     src_ref=src.at[to],
                     dst_ref=dst.at[d],
-                    send_sem=ssem.at[k],
-                    recv_sem=rsem.at[d],
+                    send_sem=ssem.at[0],
+                    recv_sem=rsem.at[0],
                     device_id={"dp": to},
                     device_id_type=MESH,
                 )
                 copy.start()
-                copies.append(copy)
         dst[d] = src[d]
-        return copies
+
+    def all_of(axis, size, me, src, dst, ssem, rsem):
+        return pltpu.make_async_remote_copy(
+            src_ref=src.at[pl.ds(0, size - 1)],
+            dst_ref=dst.at[pl.ds(0, size - 1)],
+            send_sem=ssem.at[0],
+            recv_sem=rsem.at[0],
+            device_id={axis: lax.rem(me + 1, size)},
+            device_id_type=MESH,
+        )
 
     def received(src, dst, ssem, rsem):
-        for k in range(1, ND):
-            o = lax.rem(d + k, ND)
-            pltpu.make_async_remote_copy(
-                src_ref=src.at[o],
-                dst_ref=dst.at[o],
-                send_sem=ssem.at[k],
-                recv_sem=rsem.at[o],
-                device_id={"dp": o},
-                device_id_type=MESH,
-            ).wait_recv()
+        all_of("dp", ND, d, src, dst, ssem, rsem).wait_recv()
 
     loads = []
     for i, (src, dst) in enumerate(
@@ -242,19 +263,17 @@
 
     pl.semaphore_wait(barrier, NT - 1 + ND - 1)
 
-    zcopies = []
     for k in range(1, NT):
         o = lax.rem(t + k, NT)
         copy = pltpu.make_async_remote_copy(
             src_ref=zsend.at[o],
             dst_ref=zrecv.at[t],
-            send_sem=zssem.at[k],
-            recv_sem=zrsem.at[t],
+            send_sem=zssem.at[0],
+            recv_sem=zrsem.at[0],
             device_id={"tensor": o},
             device_id_type=MESH,
         )
         copy.start()
-        zcopies.append(copy)
     zrecv[t] = zsend[t]
 
     wwide = dot_nn(weight[...].reshape(NB * R, C), repeat)
@@ -269,16 +288,7 @@
         dpad[s] = jnp.zeros((128, N), BF16)
         vpad[s] = jnp.zeros((128, N), BF16)
 
-    for k in range(1, NT):
-        o = lax.rem(t + k, NT)
-        pltpu.make_async_remote_copy(
-            src_ref=zsend.at[o],
-            dst_ref=zrecv.at[o],
-            send_sem=zssem.at[k],
-            recv_sem=zrsem.at[o],
-            device_id={"tensor": o},
-            device_id_type=MESH,
-        ).wait_recv()
+    all_of("tensor", NT, t, zsend, zrecv, zssem, zrsem).wait_recv()
 
     for k in range(4):
         tiles = [zrecv[4 * k + j].astype(F32) for j in range(4)]
@@ -312,8 +322,9 @@
     for s in range(NS):
         tall[group_at(s), :] = dot_nn(gbuf[d, s], qr[s])
     hsend[...] = tall[...].T.astype(BF16).reshape(ND, R, 128)
-    hcopies = exchange(hsend, hrecv, hssem, hrsem)
-    gather.along_y()
+    exchange(hsend, hrecv, hssem, hrsem)
+    gather.begin()
+    gather.ring(1)
 
     loads[0].wait()
     received(hsend, hrecv, hssem, hrsem)
@@ -324,9 +335,9 @@
         tall[group_at(s), :] = high
         tall[group_at(s + 3), :] = turned - high
     rsend[...] = tall[...].T.astype(BF16).reshape(ND, R, 128)
-    rcopies = exchange(rsend, rrecv, rssem, rrsem)
-    for i in range(4):
-        gather.along_x(i)
+    exchange(rsend, rrecv, rssem, rrsem)
+    gather.ring(2)
+    gather.ring(3)
 
     for i in range(2, 4):
         loads[i].wait()
@@ -350,10 +361,11 @@
         turned = turned + dot_nt(qr[s], dpad[s])
     bsend[...] = turned.astype(BF16).reshape(ND, R, 128)
 
-    bcopies = exchange(bsend, brecv, bssem, brsem)
-
-    for i in range(4, 8):
-        gather.along_x(i)
+    exchange(bsend, brecv, bssem, brsem)
+
+    gather.ring(4)
+    for i in range(4):
+        gather.onward(i)
 
     received(bsend, brecv, bssem, brsem)
 
@@ -364,39 +376,42 @@
     for s in range(1, NS):
         update = update + dot_nt(ql[s], vpad[s])
     usend[...] = update.astype(BF16).reshape(ND, R, 128)
-    ucopies = exchange(usend, urecv, ussem, ursem)
-
-    for i in range(8):
+    exchange(usend, urecv, ussem, ursem)
+
+    for i in range(4, 8):
         gather.onward(i)
 
     received(usend, urecv, ussem, ursem)
 
     for o in range(NT):
         ysend[o] = (urecv[2 * o].astype(F32) + urecv[2 * o + 1].astype(F32)).astype(BF16)
-    ycopies = []
     for k in range(1, NT):
         o = lax.rem(t + k, NT)
         copy = pltpu.make_async_remote_copy(
             src_ref=ysend.at[o],
             dst_ref=yrecv.at[t],
-            send_sem=yssem.at[k],
-            recv_sem=yrsem.at[t],
+            send_sem=yssem.at[0],
+            recv_sem=yrsem.at[0],
             device_id={"tensor": o},
             device_id_type=MESH,
         )
         copy.start()
-        ycopies.append(copy)
     yrecv[t] = ysend[t]
-    for k in range(1, NT):
-        o = lax.rem(t + k, NT)
-        pltpu.make_async_remote_copy(
-            src_ref=ysend.at[o],
-            dst_ref=yrecv.at[o],
-            send_sem=yssem.at[k],
-            recv_sem=yrsem.at[o],
-            device_id={"tensor": o},
-            device_id_type=MESH,
-        ).wait_recv()
+
+    def whole(s):
+        return gbuf[:, s].reshape(N, N)
+
+    gather.last()
+    gram_scale = 1.0 - beta_gram
+    loads[4].wait()
+    for s in range(NS):
+        product = dot_nt(gbuf[d, s], whole(s))
+        lg[s] = beta_gram * lg[s] + gram_scale * product
+    copy = pltpu.make_async_copy(lg, nl_hbm, osem.at[2])
+    copy.start()
+    stores.append(copy)
+
+    all_of("tensor", NT, t, ysend, yrecv, yssem, yrsem).wait_recv()
 
     for k in range(NB // 4):
         tile = zero
@@ -419,19 +434,6 @@
     final = PlaneGather(wbuf, wssem, wrsem, x, y)
     final.along_x(0)
     final.along_y()
-
-    def whole(s):
-        return gbuf[:, s].reshape(N, N)
-
-    gather.last()
-    gram_scale = 1.0 - beta_gram
-    loads[4].wait()
-    for s in range(NS):
-        product = dot_nt(gbuf[d, s], whole(s))
-        lg[s] = beta_gram * lg[s] + gram_scale * product
-    copy = pltpu.make_async_copy(lg, nl_hbm, osem.at[2])
-    copy.start()
-    stores.append(copy)
 
     for i in range(1, 8):
         final.along_x(i)
@@ -470,10 +472,17 @@
         copy.start()
         stores.append(copy)
 
-    for copy in zcopies + hcopies + rcopies + bcopies + ucopies + ycopies:
-        copy.wait_send()
-    for copy in gather.started + final.started:
-        copy.wait_send()
+    for args in (
+        ("dp", ND, d, hsend, hrecv, hssem, hrsem),
+        ("dp", ND, d, rsend, rrecv, rssem, rrsem),
+        ("dp", ND, d, bsend, brecv, bssem, brsem),
+        ("dp", ND, d, usend, urecv, ussem, ursem),
+        ("tensor", NT, t, zsend, zrecv, zssem, zrsem),
+        ("tensor", NT, t, ysend, yrecv, yssem, yrsem),
+    ):
+        all_of(*args).wait_send()
+    gather.finish()
+    final.finish()
     for copy in stores:
         copy.wait()
 
@@ -536,21 +545,21 @@
             pltpu.VMEM((ND, R, NB * C), BF16),
             dma((6,)),
             dma((8,)),
-            dma((NT,)),
-            dma((NT,)),
-            dma((31,)),
+            dma((1,)),
+            dma((1,)),
+            dma((1,)),
             dma((ND,)),
-            dma((ND,)),
-            dma((ND,)),
-            dma((ND,)),
-            dma((ND,)),
-            dma((ND,)),
-            dma((ND,)),
-            dma((ND,)),
-            dma((ND,)),
-            dma((NT,)),
-            dma((NT,)),
-            dma((31,)),
+            dma((1,)),
+            dma((1,)),
+            dma((1,)),
+            dma((1,)),
+            dma((1,)),
+            dma((1,)),
+            dma((1,)),
+            dma((1,)),
+            dma((1,)),
+            dma((1,)),
+            dma((1,)),
             dma((ND,)),
         ],
         compiler_params=pltpu.CompilerParams(

time: 84.5 us -> 76.6 us (0.907)
  Pallas kernels: 83.7 us -> 75.8 us
    pallas_call x1, Pallas kernels: 81.5 us -> 73.6 us  [per_device(): pl.pallas_call(kernel, out_shape=(jax.ShapeDtypeStruct((NB * C, N), BF16)...]
where the time goes in v4:
time: 76.6 us; the launch traced here: 76.4 us
  Pallas kernels  75.8 us (99%)
    pallas_call x1, Pallas kernels, per_device(): pl.pallas_call(kernel, out_shape=(jax.ShapeDtypeStruct((NB * C, N), BF16)...  73.6 us
    pallas_call x1, Pallas kernels, per_device(): pl.pallas_call(hand_over, out_shape=(jax.ShapeDtypeStruct((NB * C, N), BF...  2.16 us

profile of v4, /device:TPU:6, one launch (start us, length us, event | category | flops | bytes accessed | tf_op | source)
XLA Modules:
  0.0 76.4 jit_solution(5459370028097834163)
XLA Ops:
  0.6 73.6 %soap_step.1 = (bf16[768,512]{1,0:T(8,128)(2,1)}, f32[3,16,512]{2,1,0:T(8,128)}, f32[3,16,512]{2,1,0:T(8,128)}, f32[3,16,512]{2,1,0:T(8,128)}, f32[3,16,512]{2,1,0:T(8,128)}) custom-call(s32[24]{0:T(128)} %bitcast.4, bf16[24,16,32]{2,1,0:T(8,128)(2,1)} %grad.1, bf16[24,16,32]{2,1,0:T(8,128)(2,1)} %weight.1, bf16[3,512,512]{2,1,0:T(8,128)(2,1)} %ql_hbm.1, ...), custom_call_target="tpu_custom_call" | custom-call | tf_op jit(solution)/shard_map/soap_step/pallas_call | solution.py:514
  74.3 2.2 %hand_over.1 = (bf16[768,512]{1,0:T(8,128)(2,1)}, f32[3,16,512]{2,1,0:T(8,128)}, f32[3,16,512]{2,1,0:T(8,128)}, f32[3,16,512]{2,1,0:T(8,128)}, f32[3,16,512]{2,1,0:T(8,128)}) custom-call(bf16[768,512]{1,0:T(8,128)(2,1)} %get-tuple-element.15.w, f32[3,16,512]{2,1,0:T(8,128)} %get-tuple-element.16.nl, f32[3,16,512]{2,1,0:T(8,128)} %get-tuple-element.17.nr, ...), custom_call_target="tpu_custom_call" | custom-call | tf_op jit(solution)/shard_map/hand_over/pallas_call | solution.py:570

commit v5 on v4

--- a/solution.py
+++ b/solution.py
@@ -39,12 +39,12 @@
 class PlaneGather:
     legs = (1, -1, 2, -2, 3, -3, 4)
 
-    def __init__(self, buf, ssem, rsem, x, y):
-        self.buf, self.ssem, self.rsem, self.x, self.y = buf, ssem, rsem, x, y
+    def __init__(self, buf, ssem, rsem, xs, ys):
+        self.buf, self.ssem, self.rsem, self.xs, self.ys = buf, ssem, rsem, xs, ys
         self.started = []
 
     def place(self, dx, dy):
-        return lax.rem(self.x + dx + NX, NX) * NY + lax.rem(self.y + dy + NY, NY)
+        return self.xs[dx % NX] + self.ys[dy % NY]
 
     def copy_of(self, dx, dy, tx, ty):
         src = self.place(dx, dy)
@@ -187,6 +187,8 @@
     t = lax.axis_index("tensor")
     x = d // NY
     y = lax.rem(d, NY)
+    xs = [lax.rem(x + k, NX) * NY for k in range(NX)]
+    ys = [lax.rem(y + k, NY) for k in range(NY)]
 
     barrier = pltpu.get_barrier_semaphore()
     for k in range(1, NT):
@@ -195,7 +197,7 @@
         )
     for k in range(1, ND):
         pl.semaphore_signal(
-            barrier, inc=1, device_id={"dp": lax.rem(d + k, ND)}, device_id_type=MESH
+            barrier, inc=1, device_id={"dp": xs[k // NY] + ys[k % NY]}, device_id_type=MESH
         )
 
     def exchange(src, dst, ssem, rsem):
@@ -203,7 +205,7 @@
             for dy in (4, 3, 5, 2, 6, 1, 7, 0):
                 if dx == 0 and dy == 0:
                     continue
-                to = lax.rem(x + dx, NX) * NY + lax.rem(y + dy, NY)
+                to = xs[dx] + ys[dy]
                 copy = pltpu.make_async_remote_copy(
                     src_ref=src.at[to],
                     dst_ref=dst.at[d],
@@ -300,7 +302,7 @@
                 tile = pltpu.roll(tile, 128 - 32 * s, 1)
             gbuf[d, s, :, 128 * k : 128 * (k + 1)] = tile.astype(BF16)
 
-    gather = PlaneGather(gbuf, gssem, grsem, x, y)
+    gather = PlaneGather(gbuf, gssem, grsem, xs, ys)
     m = lax.rem(d, 8)
     h = lax.rem(d, 2)
 
@@ -315,13 +317,36 @@
             parts.append(tile)
         return jnp.concatenate(parts, axis=1)
 
+    half16 = lax.broadcasted_iota(jnp.int32, (R // 2, 128), 1) // 16
+
+    def fold(turned):
+        tiles = turned.reshape(ND, R, 128)
+        low = pltpu.roll(tiles[:, R // 2 :].reshape(ND * R // 2, 128), 48, 1)
+        folded = tiles[:, : R // 2].reshape(ND * R // 2, 128) + low
+        return folded.astype(BF16).reshape(ND, R // 2, 128)
+
+    def unfold(src, offset):
+        parts = []
+        for k in range(4):
+            halves = []
+            for shift in (offset, offset + 3):
+                tile = jnp.zeros((R // 2, 128), F32)
+                for j in range(8):
+                    chosen = half16 == (j + shift) % 8
+                    tile = jnp.where(chosen, src[8 * k + j].astype(F32), tile)
+                if shift:
+                    tile = pltpu.roll(tile, 128 - 16 * shift, 1)
+                halves.append(tile)
+            parts.append(jnp.concatenate(halves, axis=0))
+        return jnp.concatenate(parts, axis=1)
+
     def group_at(offset):
         return pl.ds(pl.multiple_of(16 * lax.rem(m + offset, 8), 16), 16)
 
     loads[1].wait()
     for s in range(NS):
         tall[group_at(s), :] = dot_nn(gbuf[d, s], qr[s])
-    hsend[...] = tall[...].T.astype(BF16).reshape(ND, R, 128)
+    hsend[...] = fold(tall[...].T)
     exchange(hsend, hrecv, hssem, hrsem)
     gather.begin()
     gather.ring(1)
@@ -329,7 +354,7 @@
     loads[0].wait()
     received(hsend, hrecv, hssem, hrsem)
     for s in range(NS):
-        half = lane_groups(hrecv, s).astype(BF16)
+        half = unfold(hrecv, s).astype(BF16)
         turned = dot_nn(half, ql[s])
         high = turned.astype(BF16).astype(F32)
         tall[group_at(s), :] = high
@@ -359,7 +384,7 @@
     turned = dot_nt(qr[0], dpad[0])
     for s in range(1, NS):
         turned = turned + dot_nt(qr[s], dpad[s])
-    bsend[...] = turned.astype(BF16).reshape(ND, R, 128)
+    bsend[...] = fold(turned)
 
     exchange(bsend, brecv, bssem, brsem)
 
@@ -371,7 +396,7 @@
 
     for s in range(NS):
         at = pl.multiple_of(32 * s + 16 * h, 16)
-        vpad[s, pl.ds(at, 16), :] = lane_groups(brecv, s).astype(BF16)
+        vpad[s, pl.ds(at, 16), :] = unfold(brecv, s).astype(BF16)
     update = dot_nt(ql[0], vpad[0])
     for s in range(1, NS):
         update = update + dot_nt(ql[s], vpad[s])
@@ -431,7 +456,7 @@
         1.0,
         0.0,
     ).astype(BF16)
-    final = PlaneGather(wbuf, wssem, wrsem, x, y)
+    final = PlaneGather(wbuf, wssem, wrsem, xs, ys)
     final.along_x(0)
     final.along_y()
 
@@ -530,13 +555,13 @@
             pltpu.VMEM((NT, R, 128), BF16),
             pltpu.VMEM((ND, NS, R, N), BF16),
             pltpu.VMEM((128, N), F32),
-            pltpu.VMEM((ND, R, 128), BF16),
-            pltpu.VMEM((ND, R, 128), BF16),
+            pltpu.VMEM((ND, R // 2, 128), BF16),
+            pltpu.VMEM((ND, R // 2, 128), BF16),
             pltpu.VMEM((ND, R, 128), BF16),
             pltpu.VMEM((ND, R, 128), BF16),
             pltpu.VMEM((NS, 128, N), BF16),
-            pltpu.VMEM((ND, R, 128), BF16),
-            pltpu.VMEM((ND, R, 128), BF16),
+            pltpu.VMEM((ND, R // 2, 128), BF16),
+            pltpu.VMEM((ND, R // 2, 128), BF16),
             pltpu.VMEM((NS, 128, N), BF16),
             pltpu.VMEM((ND, R, 128), BF16),
             pltpu.VMEM((ND, R, 128), BF16),

time: 76.6 us -> 75.9 us (level)
  Pallas kernels: 75.8 us -> 74.7 us
    pallas_call x1, Pallas kernels: 73.6 us -> 72.5 us  [per_device(): pl.pallas_call(kernel, out_shape=(jax.ShapeDtypeStruct((NB * C, N), BF16)...]
where the time goes in v5:
time: 75.9 us; the launch traced here: 75.3 us
  Pallas kernels  74.7 us (98%)
    pallas_call x1, Pallas kernels, per_device(): pl.pallas_call(kernel, out_shape=(jax.ShapeDtypeStruct((NB * C, N), BF16)...  72.5 us
    pallas_call x1, Pallas kernels, per_device(): pl.pallas_call(hand_over, out_shape=(jax.ShapeDtypeStruct((NB * C, N), BF...  2.16 us

profile of v5, /device:TPU:6, one launch (start us, length us, event | category | flops | bytes accessed | tf_op | source)
XLA Modules:
  0.0 75.3 jit_solution(6427725061671957595)
XLA Ops:
  0.6 72.5 %soap_step.1 = (bf16[768,512]{1,0:T(8,128)(2,1)}, f32[3,16,512]{2,1,0:T(8,128)}, f32[3,16,512]{2,1,0:T(8,128)}, f32[3,16,512]{2,1,0:T(8,128)}, f32[3,16,512]{2,1,0:T(8,128)}) custom-call(s32[24]{0:T(128)} %bitcast.4, bf16[24,16,32]{2,1,0:T(8,128)(2,1)} %grad.1, bf16[24,16,32]{2,1,0:T(8,128)(2,1)} %weight.1, bf16[3,512,512]{2,1,0:T(8,128)(2,1)} %ql_hbm.1, ...), custom_call_target="tpu_custom_call" | custom-call | tf_op jit(solution)/shard_map/soap_step/pallas_call | solution.py:539
  73.2 2.2 %hand_over.1 = (bf16[768,512]{1,0:T(8,128)(2,1)}, f32[3,16,512]{2,1,0:T(8,128)}, f32[3,16,512]{2,1,0:T(8,128)}, f32[3,16,512]{2,1,0:T(8,128)}, f32[3,16,512]{2,1,0:T(8,128)}) custom-call(bf16[768,512]{1,0:T(8,128)(2,1)} %get-tuple-element.15.w, f32[3,16,512]{2,1,0:T(8,128)} %get-tuple-element.16.nl, f32[3,16,512]{2,1,0:T(8,128)} %get-tuple-element.17.nr, ...), custom_call_target="tpu_custom_call" | custom-call | tf_op jit(solution)/shard_map/hand_over/pallas_call | solution.py:595
